TPU v7x, 32 devices: a whole 2x2x4 slice. The times are simulated.
32 devices in a mesh: line: 16 (over z, x, core), bus: 2 (over y).
Axes of the slice: x: 2, y: 2, z: 4, core: 2. Of those that a mesh axis runs over, the one named last changes fastest.
Arguments:
- injections: float32 [1024, 8192], P('line', 'bus'), may hold values from -6 to 6
- shift_factors: float32 [16384, 8192], P('line', 'bus'), may hold values from -0.0625 to 0.0625
- line_rating: int32 [1024, 16384], P(None, 'line'), may hold values from 40 to 159
- retention: float32 [1024, 256], P('line', 'bus'), may hold values from 0.5 to 1
- discharge: float32 [256], P('bus'), may hold values from 0.05 to 0.5
- profile: float32 [1024, 256], P('line', 'bus'), may hold values from -6 to 6
- storage_bus: int32 [256], P('bus'), may hold values from 0 to 8191, as said below
- online_hour: int32 [256], P('bus'), may hold values from 0 to 511
Outputs:
- bus_adjoint: float32 [1024, 8192], P('line', 'bus')
- size_grad: float32 [256], P('bus')
Inputs may be any that keep to these rules, and one draw needn't show every extreme that they name: `storage_bus`: unit k sits at a bus of index from (k // 128) * 4096 to (k // 128 + 1) * 4096 - 1.
All inputs are finite; a program needn't handle non-finite values.
Results may differ from a plain program's by a relative error of at most 0.0003.
Values sent between devices are 32-bit elements; how exact they have to be, the bound alone decides.
A program may use at most 128 MiB of HBM per device.

v0:
```python
import math

import jax
import jax.numpy as jnp
from jax import lax
from jax.sharding import PartitionSpec as P


def entering(shard, axis, combine, identity):
    length, index = (lax.axis_size(axis), lax.axis_index(axis))
    everything = jax.tree.map(lambda part: lax.all_gather(part, axis), shard)
    start = jax.tree.map(
        lambda part, zero: jnp.broadcast_to(jnp.asarray(zero, part.dtype), part.shape),
        shard,
        identity,
    )

    def turn(k, before):
        at = length - 1 - k
        reached = at > index
        new = combine(before, jax.tree.map(lambda part: part[at], everything))
        return jax.tree.map(lambda a, b: jnp.where(reached, a, b), new, before)

    return lax.fori_loop(0, length, turn, start)


def overload(line_flows, limits):
    excess = jnp.maximum(jnp.abs(line_flows) - limits, 0.0)
    return excess * jnp.sign(line_flows)


def combine(earlier, latter):
    return (latter[0] * earlier[0], latter[1] + latter[0] * earlier[1])


def total_overload(partial_flows, limits):
    flow_share = lax.psum_scatter(partial_flows, "bus", scatter_dimension=1, tiled=True)
    share_width = flow_share.shape[1]
    limit_share = lax.dynamic_slice_in_dim(
        limits, lax.axis_index("bus") * share_width, share_width, 1
    )
    return lax.all_gather(overload(flow_share, limit_share), "bus", axis=1, tiled=True)


def on_device(
    injections, shift_factors, line_rating, retention, discharge, profile, storage_bus, online_hour
):
    highest = lax.Precision.HIGHEST
    hour_dev = injections.shape[0]
    line_count = lax.axis_size("line")
    hours = hour_dev * line_count
    bus_dev = shift_factors.shape[1]
    store_dev = retention.shape[1]
    line_pos = lax.axis_index("line")
    partial_flows = lax.dot_general(
        lax.all_gather(injections, "line", axis=0, tiled=True),
        shift_factors,
        (((1,), (1,)), ((), ())),
        precision=highest,
        preferred_element_type=jnp.float32,
    )
    limits = line_rating.astype(jnp.float32) * 0.01
    flow_adjoint = total_overload(partial_flows, limits)
    bus_adjoint = lax.psum_scatter(
        jnp.dot(flow_adjoint, shift_factors, precision=highest, preferred_element_type=jnp.float32),
        "line",
        scatter_dimension=0,
        tiled=True,
    )
    local_bus = storage_bus - lax.axis_index("bus") * bus_dev
    onehot = (jnp.arange(bus_dev, dtype=jnp.int32)[:, None] == local_bus[None, :]).astype(
        jnp.float32
    )
    source = discharge[None, :] * jnp.dot(
        bus_adjoint, onehot, precision=highest, preferred_element_type=jnp.float32
    )
    next_keep = jnp.concatenate([retention[1:], jnp.ones((1, store_dev), jnp.float32)], axis=0)
    composed = lax.associative_scan(combine, (next_keep[::-1], source[::-1]), axis=0)
    gain_local = composed[0][::-1]
    offset_local = composed[1][::-1]
    block_gain = retention[0] * gain_local[0]
    block_offset = retention[0] * offset_local[0]
    identity = (jnp.ones((store_dev,), jnp.float32), jnp.zeros((store_dev,), jnp.float32))
    carried = entering((block_gain, block_offset), "line", combine, identity)
    carried_in = carried[1]
    costate = offset_local + gain_local * carried_in[None, :]
    hour_index = line_pos * hour_dev + jnp.arange(hour_dev, dtype=jnp.int32)
    active = (hour_index[:, None] >= online_hour[None, :]).astype(jnp.float32)
    partial_size = jnp.sum(costate * profile * active, axis=0) / math.sqrt(hours)
    size_grad = lax.psum(partial_size, "line")
    return (bus_adjoint, size_grad)


def solution(mesh):
    in_specs = (
        P("line", "bus"),
        P("line", "bus"),
        P(None, "line"),
        P("line", "bus"),
        P("bus"),
        P("line", "bus"),
        P("bus"),
        P("bus"),
    )
    out_specs = (P("line", "bus"), P("bus"))
    return jax.shard_map(
        on_device, mesh=mesh, in_specs=in_specs, out_specs=out_specs, check_vma=False
    )
```

profile of v0, /device:TPU:0, one launch (start us, length us, event | category | flops | bytes accessed | tf_op | source)
XLA Modules:
  0.0 629.5 jit_solution(8625061213054991973)
XLA Ops:
  7.2 0.0 all-gather.5.cloned.1.call-start
  7.2 0.7 all-gather.5.cloned.1.call-update
  7.9 0.0 reduce-scatter.3.cloned.1.call-start
  7.9 131.8 %all-gather.5.cloned.1.call-done = f32[1024,4096]{1,0:T(8,128)} async-done(((f32[64,4096]{1,0:T(8,128)}), f32[1024,4096]{1,0:T(8,128)}) %all-gather.5.cloned.1.call-update) | async-done | bytes 16777232 | tf_op jit(solution)/shard_map/all_gather | solution.py:56
  139.8 59.5 %fusion.18 = f32[1024,1024]{1,0:T(8,128)} fusion(f32[1024,4096]{1,0:T(8,128)} %all-gather.5.cloned.1.call-done, f32[1024,4096]{1,0:T(8,128)} %param.11), kind=kOutput, calls=%fused_computation.57 | convolution fusion | flops 51539607552 | bytes 37748736 | tf_op jit(solution)/shard_map/dot_general | solution.py:55
  199.3 0.0 reduce-scatter.3.cloned.1.call-update
  199.3 0.0 all-gather.7.cloned.1.call-start
  199.4 52.6 %reduce-scatter.3.cloned.1.call-done = f32[1024,512]{1,0:T(8,128)} async-done(((f32[1024,1024]{1,0:T(8,128)}), f32[1024,512]{1,0:T(8,128)}) %reduce-scatter.3.cloned.1.call-update) | async-done | bytes 2097168 | tf_op jit(solution)/shard_map/reduce_scatter | solution.py:37
  251.9 4.4 fusion.4
  256.4 0.0 all-gather.7.cloned.1.call-update
  256.4 0.2 reduce-scatter.5.cloned.1.call-start
  256.6 56.7 %all-gather.7.cloned.1.call-done = f32[1024,1024]{1,0:T(8,128)} async-done(((f32[1024,512]{1,0:T(8,128)}), f32[1024,1024]{1,0:T(8,128)}) %all-gather.7.cloned.1.call-update) | async-done | bytes 4194320 | tf_op jit(solution)/shard_map/all_gather | solution.py:42
  313.3 58.4 %fusion.19 = f32[1024,4096]{1,0:T(8,128)} fusion(f32[1024,1024]{1,0:T(8,128)} %all-gather.7.cloned.1.call-done, f32[1024,4096]{1,0:T(8,128)} %param.11), kind=kOutput, calls=%fused_computation.58 | convolution fusion | flops 51539607552 | bytes 37748736 | tf_op jit(solution)/shard_map/dot_general | solution.py:65
  371.7 0.0 copy-start
  371.7 0.0 copy-start.4
  371.7 0.0 copy-start.2
  371.7 0.0 copy-start.1
  371.8 0.0 copy-start.3
  371.8 0.0 reduce-scatter.5.cloned.1.call-update
  371.8 0.7 copy-done
  372.6 0.0 copy-done.4
  372.7 177.9 %reduce-scatter.5.cloned.1.call-done = f32[64,4096]{1,0:T(8,128)} async-done(((f32[1024,4096]{1,0:T(8,128)}), f32[64,4096]{1,0:T(8,128)}) %reduce-scatter.5.cloned.1.call-update) | async-done | bytes 1048592 | tf_op jit(solution)/shard_map/reduce_scatter | solution.py:64
  550.5 0.0 copy-done.2
  550.5 2.2 fusion.6
  553.9 19.3 %all-gather = f32[16,1,128]{2,1,0:T(1,128)S(1)} all-gather(f32[1,1,128]{2,1,0:T(1,128)S(1)} %get-tuple-element.164), channel_id=1, replica_groups=mesh['line'=16,'bus'=2] {'line'}, dimensions={0}, use_global_device_ids=true | all-gather | bytes 8704 | tf_op jit(solution)/shard_map/all_gather | solution.py:11
  573.2 17.3 %all-gather.1 = f32[16,1,128]{2,1,0:T(1,128)S(1)} all-gather(f32[1,1,128]{2,1,0:T(1,128)S(1)} %get-tuple-element.163), channel_id=1, replica_groups=mesh['line'=16,'bus'=2] {'line'}, dimensions={0}, use_global_device_ids=true | all-gather | bytes 8704 | tf_op jit(solution)/shard_map/all_gather | solution.py:11
  590.5 0.7 while.16
  591.3 0.0 copy-done.1
  591.3 0.0 copy-done.3
  591.3 0.1 select_reduce_fusion
  591.4 31.6 %psum.7 = f32[128]{0:T(128)} all-reduce(f32[128]{0:T(128)S(1)} %broadcast_multiply_fusion), channel_id=1, replica_groups=mesh['line'=16,'bus'=2] {'line'}, use_global_device_ids=true, to_apply=%region_5.6 | all-reduce | flops 128 | bytes 1024 | tf_op jit(solution)/shard_map/psum | solution.py:90
  (118 shorter events, 1.3 us)
Async XLA Ops:
  7.2 132.6 %all-gather.5.cloned.1.call-start = ((), (), s32[]{:S(2)}) async-start(), calls=%async_computation.2 | async-start | bytes 17825792 | tf_op jit(solution)/shard_map/all_gather | solution.py:56
  7.9 244.0 %reduce-scatter.3.cloned.1.call-start = ((), (), s32[]{:S(2)}) async-start(), calls=%async_computation.3 | async-start | bytes 6291456 | tf_op jit(solution)/shard_map/reduce_scatter | solution.py:37
  199.3 114.0 %all-gather.7.cloned.1.call-start = ((), (), s32[]{:S(2)}) async-start(), calls=%async_computation.4 | async-start | bytes 6291456 | tf_op jit(solution)/shard_map/all_gather | solution.py:42
  256.4 294.1 %reduce-scatter.5.cloned.1.call-start = ((), (), s32[]{:S(2)}) async-start(), calls=%async_computation.5 | async-start | bytes 17825792 | tf_op jit(solution)/shard_map/reduce_scatter | solution.py:64
  371.7 0.8 copy-start
  371.7 0.9 copy-start.4
  371.7 178.8 %copy-start.2 = (f32[128]{0:T(128)S(1)}, f32[128]{0:T(128)}, u32[]{:S(2)}) copy-start(f32[128]{0:T(128)} %param.14) | copy-start | bytes 1540
  371.7 219.5 %copy-start.1 = (f32[64,128]{1,0:T(8,128)S(1)}, f32[64,128]{1,0:T(8,128)}, u32[]{:S(2)}) copy-start(f32[64,128]{1,0:T(8,128)} %param.15) | copy-start | bytes 98308
  371.8 219.5 %copy-start.3 = (s32[128]{0:T(128)S(1)}, s32[128]{0:T(128)}, u32[]{:S(2)}) copy-start(s32[128]{0:T(128)} %param.17) | copy-start | bytes 1540
Sparse Core Ops, SparseCore 0:
  10.2 129.5 all-gather.4
  199.4 52.4 reduce-scatter.2
  256.5 56.7 all-gather.6
  371.9 178.5 reduce-scatter.4
where the time goes:
time: 630 us
  waiting for transfers between devices  420 us (67%)
  matrix products  120 us (19%)
  blocking collectives  68.2 us (11%)
  between operations  14.3 us (2%)
    reduce_scatter x1, waiting for transfers between devices, on_device(): lax.psum_scatter(jnp.dot(flow_adjoint, shift_factors, precision=highest,...  178 us
    all_gather x1, waiting for transfers between devices, on_device(): lax.all_gather(injections, 'line', axis=0, tiled=True)  132 us
    dot_general x1, matrix products, on_device(): lax.dot_general(lax.all_gather(injections, 'line', axis=0, tiled=True), s...  59.5 us
    dot_general x1, matrix products, on_device(): jnp.dot(flow_adjoint, shift_factors, precision=highest, preferred_element...  58.4 us
    all_gather x1, waiting for transfers between devices, total_overload(): lax.all_gather(overload(flow_share, limit_share), 'bus', axis=1, tiled=True)  56.7 us
    reduce_scatter x1, waiting for transfers between devices, total_overload(): lax.psum_scatter(partial_flows, 'bus', scatter_dimension=1, tiled=True)  52.6 us
    all_gather x2, blocking collectives, entering(): everything = jax.tree.map(lambda part: lax.all_gather(part, axis), shard)  36.6 us
    psum x1, blocking collectives, on_device(): size_grad = lax.psum(partial_size, 'line')  31.6 us
  transfers between devices with their start and end apart: 4, of which 4 were waited for; matrix products, arithmetic and copies ran while one was open for 0% of the time, Pallas kernels for 0%

commit v1 on v0

v1 whole, which is shorter than its diff:
```python
import functools
import math

import jax
import jax.numpy as jnp
from jax import lax
from jax.experimental import pallas as pl
from jax.experimental.pallas import tpu as pltpu
from jax.sharding import PartitionSpec as P

MESH = pl.DeviceIdType.MESH
F32, BF16 = jnp.float32, jnp.bfloat16


def split(value):
    high = value.astype(BF16)
    return high, (value - high.astype(F32)).astype(BF16)


def dot3(a_hi, a_lo, b_hi, b_lo, dims):
    dot = functools.partial(
        lax.dot_general, dimension_numbers=(dims, ((), ())), preferred_element_type=F32
    )
    return dot(a_hi, b_hi) + (dot(a_hi, b_lo) + dot(a_lo, b_hi))


def tile_of(width, most):
    return math.gcd(width, most)


def kernel(
    planes, bus_count,
    inj, factors, rating, retention, discharge, profile, local_bus, online,
    out, stats, gathered,
    s_hi, s_lo, stage, x_hi, x_lo, flows, flows_in, a_hi, a_lo, limit, part,
    from_core, from_x, from_z, source,
    local_sem,
    gz_send, gz_recv, gx_send, gx_recv, gc_send, gc_recv,
    y_send, y_recv, rc_send, rc_recv, rx_send, rx_recv, rz_send, rz_recv,
):
    line, bus = lax.axis_index("line"), lax.axis_index("bus")
    z, x, c = line // 4, (line // 2) % 2, line % 2
    me = 2 * x + c
    hours, buses = inj.shape
    lines = factors.shape[0]
    chunk = 4 * hours

    def at(plane, column, core):
        return (plane * 4 + column * 2 + core, bus)

    sibling, across = at(z, x, 1 - c), at(z, 1 - x, c)

    def plane_of(s):
        both = jnp.minimum(z, planes - 1 - z)
        away = (s + 1) // 2
        near = jnp.where(s % 2 == 1, z - away, z + away)
        far = jnp.where(z < planes - 1 - z, s, planes - 1 - s)
        return jnp.where(s <= 2 * both, near, far)

    def rows(block):
        return pl.ds(pl.multiple_of(block * hours, hours), hours)

    def block_copy(plane, block, send, recv, target):
        ref = gathered.at[plane, rows(block)]
        return pltpu.make_async_remote_copy(
            src_ref=ref, dst_ref=ref, send_sem=send, recv_sem=recv,
            device_id=target, device_id_type=MESH,
        )

    def along_z(plane, way, target_plane):
        return block_copy(
            plane, me, gz_send.at[way, plane], gz_recv.at[plane], at(target_plane, x, c)
        )

    def to_across(plane):
        return block_copy(plane, me, gx_send.at[plane], gx_recv.at[plane], across)

    def from_across(plane):
        return block_copy(
            plane, 2 * (1 - x) + c, gx_send.at[plane], gx_recv.at[plane], across
        )

    def to_sibling(plane, k):
        block = 2 * (x if k == 0 else 1 - x) + c
        return block_copy(plane, block, gc_send.at[k, plane], gc_recv.at[k, plane], sibling)

    def from_sibling(plane, k):
        block = 2 * (x if k == 0 else 1 - x) + 1 - c
        return block_copy(plane, block, gc_send.at[k, plane], gc_recv.at[k, plane], sibling)

    def goes_up(plane):
        return (plane <= z) & (z + 1 < planes)

    def goes_down(plane):
        return (plane >= z) & (z > 0)

    def forward(s):
        plane = plane_of(s)

        @pl.when(s > 0)
        def _():
            along_z(plane, 0, z).wait_recv()

        @pl.when(goes_up(plane))
        def _():
            along_z(plane, 0, z + 1).start()

        @pl.when(goes_down(plane))
        def _():
            along_z(plane, 1, z - 1).start()

        to_across(plane).start()
        to_sibling(plane, 0).start()

    def forward_across(s):
        plane = plane_of(s)
        from_across(plane).wait_recv()
        to_sibling(plane, 1).start()

    def flow_copy(s, r):
        return pltpu.make_async_remote_copy(
            src_ref=flows.at[s], dst_ref=flows_in.at[s, r - 1],
            send_sem=y_send.at[s, r - 1], recv_sem=y_recv.at[s, r - 1],
            device_id=(line, (bus + r) % bus_count), device_id_type=MESH,
        )

    def first_product(s):
        plane = plane_of(s)
        from_sibling(plane, 0).wait_recv()
        from_sibling(plane, 1).wait_recv()
        load = pltpu.make_async_copy(gathered.at[plane], stage, local_sem.at[0])
        load.start()
        load.wait()
        step = tile_of(chunk, 32)

        @pl.loop(0, chunk // step)
        def _(i):
            here = pl.ds(pl.multiple_of(i * step, step), step)
            x_hi[here], x_lo[here] = split(stage[here])

        width = tile_of(lines, 256)

        @pl.loop(0, lines // width)
        def _(n):
            here = pl.ds(pl.multiple_of(n * width, width), width)
            flows[s, :, here] = dot3(
                x_hi[...], x_lo[...], s_hi[here], s_lo[here], ((1,), (1,))
            )

        for r in range(1, bus_count):
            flow_copy(s, r).start()

    def core_copy(s, k):
        return pltpu.make_async_remote_copy(
            src_ref=part.at[2 * k + 1 - c], dst_ref=from_core.at[s, k],
            send_sem=rc_send.at[s, k], recv_sem=rc_recv.at[s, k],
            device_id=sibling, device_id_type=MESH,
        )

    def x_copy(s):
        return pltpu.make_async_remote_copy(
            src_ref=from_core.at[s, 1 - x], dst_ref=from_x.at[s],
            send_sem=rx_send.at[s], recv_sem=rx_recv.at[s],
            device_id=across, device_id_type=MESH,
        )

    def z_copy(s):
        plane = plane_of(s)
        return pltpu.make_async_remote_copy(
            src_ref=from_x.at[s], dst_ref=from_z.at[z],
            send_sem=rz_send.at[s], recv_sem=rz_recv.at[z],
            device_id=at(plane, x, c), device_id_type=MESH,
        )

    def second_product(s):
        plane = plane_of(s)
        here = pl.ds(pl.multiple_of(plane * chunk, chunk), chunk)
        load = pltpu.make_async_copy(rating.at[here], limit, local_sem.at[0])
        load.start()
        for r in range(1, bus_count):
            flow_copy(s, r).wait_recv()
        load.wait()
        step = tile_of(chunk, 32)

        @pl.loop(0, chunk // step)
        def _(i):
            here = pl.ds(pl.multiple_of(i * step, step), step)
            total = flows[s, here]
            for r in range(1, bus_count):
                total = total + flows_in[s, r - 1, here]
            bound = limit[here].astype(F32) * 0.01
            adjoint = jnp.where(
                total > bound, total - bound, jnp.where(total < -bound, total + bound, 0.0)
            )
            a_hi[here], a_lo[here] = split(adjoint)

        width = tile_of(buses, 512)

        @pl.loop(0, buses // width)
        def _(n):
            here = pl.ds(pl.multiple_of(n * width, width), width)
            value = dot3(a_hi[...], a_lo[...], s_hi[:, here], s_lo[:, here], ((1,), (0,)))
            for block in range(4):
                part[block, :, here] = value[block * hours : (block + 1) * hours]

        for k in range(2):
            core_copy(s, k).start()

    def add_to(ref, *others):
        step = tile_of(hours, 8)

        @pl.loop(0, hours // step)
        def _(i):
            here = pl.ds(pl.multiple_of(i * step, step), step)
            total = ref[here]
            for other in others:
                total = total + other[here]
            ref[here] = total

    def reduce_across(s):
        for k in range(2):
            core_copy(s, k).wait_recv()
        add_to(from_core.at[s, 1 - x], part.at[2 * (1 - x) + c])
        x_copy(s).start()
        add_to(from_core.at[s, x], part.at[me])
        for k in range(2):
            core_copy(s, k).wait_send()

    def reduce_along(s):
        x_copy(s).wait_recv()
        add_to(from_x.at[s], from_core.at[s, x])

        @pl.when(s > 0)
        def _():
            z_copy(s).start()

    barrier = pltpu.get_barrier_semaphore()
    mine = pltpu.make_async_copy(inj, gathered.at[z, rows(me)], local_sem.at[0])
    mine.start()
    for target in (sibling, across):
        pl.semaphore_signal(barrier, inc=1, device_id=target, device_id_type=MESH)
    for r in range(1, planes):
        pl.semaphore_signal(
            barrier, inc=1, device_id=at((z + r) % planes, x, c), device_id_type=MESH
        )
    for r in range(1, bus_count):
        pl.semaphore_signal(
            barrier, inc=1, device_id=(line, (bus + r) % bus_count), device_id_type=MESH
        )
    mine.wait()
    pl.semaphore_wait(barrier, planes + bus_count)
    forward(0)

    group = tile_of(lines, chunk)

    def factor_load(i):
        here = pl.ds(pl.multiple_of(i * group, group), group)
        return pltpu.make_async_copy(factors.at[here], stage.at[pl.ds(0, group)], local_sem.at[0])

    @pl.loop(0, lines // group)
    def _(i):
        factor_load(i).start()
        factor_load(i).wait()
        step = tile_of(group, 16)

        @pl.loop(0, group // step)
        def _(j):
            here = pl.ds(pl.multiple_of(j * step, step), step)
            there = pl.ds(pl.multiple_of(i * group + j * step, step), step)
            s_hi[there], s_lo[there] = split(stage[here])

    @pl.loop(0, planes + 3)
    def _(t):
        @pl.when(t + 1 < planes)
        def _():
            forward(t + 1)

        @pl.when(t < planes)
        def _():
            forward_across(t)
            first_product(t)

        @pl.when((t >= 2) & (t < planes + 2))
        def _():
            s = (t - 1) % planes
            second_product(s)
            reduce_across(s)

        @pl.when(t >= 3)
        def _():
            reduce_along((t - 2) % planes)

    total = from_x.at[0]
    for r in range(1, planes):
        other = (z + r) % planes
        pltpu.make_async_remote_copy(
            src_ref=from_x.at[0], dst_ref=from_z.at[other],
            send_sem=rz_send.at[0], recv_sem=rz_recv.at[other],
            device_id=at(other, x, c), device_id_type=MESH,
        ).wait_recv()
        add_to(total, from_z.at[other])
    store = pltpu.make_async_copy(total, out, local_sem.at[0])
    store.start()

    width = tile_of(buses, 512)
    source[...] = jnp.zeros_like(source)

    @pl.loop(0, buses // width)
    def _(n):
        here = pl.ds(pl.multiple_of(n * width, width), width)
        place = n * width + lax.broadcasted_iota(jnp.int32, (width, source.shape[1]), 0)
        chosen = jnp.where(place == local_bus[...], 1.0, 0.0).astype(BF16)
        left = total[:, here]
        for _ in range(3):
            high = left.astype(BF16)
            left = left - high.astype(F32)
            source[...] += jnp.dot(high, chosen, preferred_element_type=F32)

    def hour_back(i, carried):
        carry, gain, fixed, slope = carried
        t = hours - 1 - i
        keep = retention[pl.ds(t, 1), :]
        weight = jnp.where(line * hours + t >= online[...], profile[pl.ds(t, 1), :], 0.0)
        costate = discharge[...] * source[pl.ds(t, 1), :] + carry
        return (keep * costate, keep * gain, fixed + costate * weight, slope + gain * weight)

    zero = jnp.zeros((1, source.shape[1]), F32)
    done = lax.fori_loop(0, hours, hour_back, (zero, zero + 1.0, zero, zero))
    stats[...] = jnp.zeros_like(stats)
    for i in range(4):
        stats[i : i + 1, :] = done[i]

    store.wait()

    @pl.loop(0, planes)
    def _(s):
        plane = plane_of(s)

        @pl.when(goes_up(plane))
        def _():
            along_z(plane, 0, z + 1).wait_send()

        @pl.when(goes_down(plane))
        def _():
            along_z(plane, 1, z - 1).wait_send()

        to_across(plane).wait_send()
        for k in range(2):
            to_sibling(plane, k).wait_send()
        for r in range(1, bus_count):
            flow_copy(s, r).wait_send()
        x_copy(s).wait_send()

        @pl.when(s > 0)
        def _():
            z_copy(s).wait_send()


def on_device(
    planes, bus_count,
    injections, shift_factors, line_rating, retention, discharge, profile, storage_bus, online_hour,
):
    hours, buses = injections.shape
    lines = shift_factors.shape[0]
    stores = retention.shape[1]
    chunk = 4 * hours
    all_hours = chunk * planes
    local_bus = storage_bus - lax.axis_index("bus") * buses
    hbm, vmem = pl.BlockSpec(memory_space=pl.ANY), pl.BlockSpec(memory_space=pltpu.VMEM)
    dma = pltpu.SemaphoreType.DMA
    bus_adjoint, stats, _ = pl.pallas_call(
        functools.partial(kernel, planes, bus_count),
        out_shape=(
            jax.ShapeDtypeStruct((hours, buses), F32),
            jax.ShapeDtypeStruct((8, stores), F32),
            jax.ShapeDtypeStruct((planes, chunk, buses), F32),
        ),
        in_specs=[hbm, hbm, hbm, vmem, vmem, vmem, vmem, vmem],
        out_specs=(hbm, vmem, hbm),
        scratch_shapes=[
            pltpu.VMEM((lines, buses), BF16),
            pltpu.VMEM((lines, buses), BF16),
            pltpu.VMEM((chunk, buses), F32),
            pltpu.VMEM((chunk, buses), BF16),
            pltpu.VMEM((chunk, buses), BF16),
            pltpu.VMEM((planes, chunk, lines), F32),
            pltpu.VMEM((planes, bus_count - 1, chunk, lines), F32),
            pltpu.VMEM((chunk, lines), BF16),
            pltpu.VMEM((chunk, lines), BF16),
            pltpu.VMEM((chunk, lines), jnp.int32),
            pltpu.VMEM((4, hours, buses), F32),
            pltpu.VMEM((planes, 2, hours, buses), F32),
            pltpu.VMEM((planes, hours, buses), F32),
            pltpu.VMEM((planes, hours, buses), F32),
            pltpu.VMEM((hours, stores), F32),
            dma((1,)),
            dma((2, planes)), dma((planes,)),
            dma((planes,)), dma((planes,)),
            dma((2, planes)), dma((2, planes)),
            dma((planes, bus_count - 1)), dma((planes, bus_count - 1)),
            dma((planes, 2)), dma((planes, 2)),
            dma((planes,)), dma((planes,)),
            dma((planes,)), dma((planes,)),
        ],
        compiler_params=pltpu.CompilerParams(
            collective_id=0, has_side_effects=True, vmem_limit_bytes=60 * 2**20
        ),
        cost_estimate=pl.CostEstimate(
            flops=12 * all_hours * lines * buses,
            bytes_accessed=4 * (lines * buses + all_hours * (buses + lines)),
            transcendentals=0,
        ),
    )(
        injections, shift_factors, line_rating, retention, discharge[None], profile,
        local_bus[None], online_hour[None],
    )
    everyone = lax.all_gather(stats, "line")
    carried = jnp.zeros((stores,), F32)
    total = jnp.zeros((stores,), F32)
    for block in reversed(range(4 * planes)):
        offset, gain, fixed, slope = (everyone[block, i] for i in range(4))
        total = total + (fixed + slope * carried)
        carried = offset + gain * carried
    return (bus_adjoint, total / math.sqrt(all_hours))


def solution(mesh):
    planes, bus_count = mesh.shape["line"] // 4, mesh.shape["bus"]
    in_specs = (
        P("line", "bus"),
        P("line", "bus"),
        P(None, "line"),
        P("line", "bus"),
        P("bus"),
        P("line", "bus"),
        P("bus"),
        P("bus"),
    )
    out_specs = (P("line", "bus"), P("bus"))
    return jax.shard_map(
        functools.partial(on_device, planes, bus_count),
        mesh=mesh, in_specs=in_specs, out_specs=out_specs, check_vma=False,
    )
```

time: 630 us -> 307 us (0.49)
  waiting for transfers between devices: 420 us -> 0 us
  Pallas kernels: 0 us -> 275 us
  matrix products: 120 us -> 0 us
  blocking collectives: 68.2 us -> 26.4 us
  between operations: 14.3 us -> 0.64 us
    pallas_call x0 -> x1, Pallas kernels: none -> 275 us  [on_device(): pl.pallas_call(functools.partial(kernel, planes, bus_count), out_shape=(j...]
    reduce_scatter x2 -> x0, waiting for transfers between devices: 230 us -> none  [the longest x1 178 us: on_device(): lax.psum_scatter(jnp.dot(flow_adjoint, shift_factors, precision=highest,...]
    all_gather x2 -> x0, waiting for transfers between devices: 189 us -> none  [the longest x1 132 us: on_device(): lax.all_gather(injections, 'line', axis=0, tiled=True)]
    dot_general x3 -> x0, matrix products: 120 us -> none  [the longest x1 59.5 us: on_device(): lax.dot_general(lax.all_gather(injections, 'line', axis=0, tiled=True), s...]
    psum x1 -> x0, blocking collectives: 31.6 us -> none  [on_device(): size_grad = lax.psum(partial_size, 'line')]
    all_gather x2 -> x1, blocking collectives: 36.6 us -> 26.4 us  [on_device(): everyone = lax.all_gather(stats, 'line')]
  transfers between devices with their start and end apart: 4 -> 0, of which waited for: 4 -> 0; matrix products, arithmetic and copies ran while one was open for 0% -> 0% of each run, Pallas kernels for 0% -> 0%
where the time goes in v1:
time: 307 us; the launch traced here: 306 us
  Pallas kernels  275 us (90%)
  blocking collectives  26.4 us (9%)
    pallas_call x1, Pallas kernels, on_device(): pl.pallas_call(functools.partial(kernel, planes, bus_count), out_shape=(j...  275 us
    all_gather x1, blocking collectives, on_device(): everyone = lax.all_gather(stats, 'line')  26.4 us

profile of v1, /device:TPU:0, one launch (start us, length us, event | category | flops | bytes accessed | tf_op | source)
XLA Modules:
  0.0 306.2 jit_solution(3233173751911803752)
XLA Ops:
  0.6 1.2 subtract_bitcast_fusion.local_bus
  1.8 275.2 %shard_map.95 = (f32[64,4096]{1,0:T(8,128)}, f32[8,128]{1,0:T(8,128)}, f32[4,256,4096]{2,1,0:T(8,128)}) custom-call(f32[64,4096]{1,0:T(8,128)} %inj.1, f32[1024,4096]{1,0:T(8,128)} %factors.1, s32[1024,1024]{1,0:T(8,128)} %rating.1, f32[64,128]{1,0:T(8,128)} %retention.1, f32[1,128]{1,0:T(1,128)} %bitcast.293, f32[64,128]{1,0:T(8,128)} %profile.1, ...), custom_call_target="tpu_custom_call" | custom-call | flops 51539607552 | bytes 37748736 | tf_op jit(solution)/shard_map/pallas_call | solution.py:371
  277.0 26.4 %all-gather = f32[128,128]{1,0:T(8,128)S(1)} all-gather(f32[8,128]{1,0:T(8,128)} %get-tuple-element.5), channel_id=2, replica_groups=mesh['line'=16,'bus'=2] {'line'}, dimensions={0}, use_global_device_ids=true | all-gather | bytes 69632 | tf_op jit(solution)/shard_map/all_gather | solution.py:417
  303.4 0.5 fusion.60
  304.0 2.3 copy.11

commit v2 on v1

--- a/solution.py
+++ b/solution.py
@@ -30,13 +30,13 @@
 
 def kernel(
     planes, bus_count,
-    inj, factors, rating, retention, discharge, profile, local_bus, online,
-    out, stats, gathered,
-    s_hi, s_lo, stage, x_hi, x_lo, flows, flows_in, a_hi, a_lo, limit, part,
-    from_core, from_x, from_z, source,
+    inj, factors, rating, retention, discharge, profile, storage_bus, online,
+    out, size, gathered,
+    s_hi, s_lo, stage, turned, flows, flows_in, a_hi, a_lo, limit, part,
+    from_core, from_x, from_z, source, all_stats,
     local_sem,
     gz_send, gz_recv, gx_send, gx_recv, gc_send, gc_recv,
-    y_send, y_recv, rc_send, rc_recv, rx_send, rx_recv, rz_send, rz_recv,
+    y_send, y_recv, rc_send, rc_recv, rx_send, rx_recv, rz_send, rz_recv, st_send, st_recv,
 ):
     line, bus = lax.axis_index("line"), lax.axis_index("bus")
     z, x, c = line // 4, (line // 2) % 2, line % 2
@@ -131,45 +131,51 @@
         load = pltpu.make_async_copy(gathered.at[plane], stage, local_sem.at[0])
         load.start()
         load.wait()
-        step = tile_of(chunk, 32)
-
-        @pl.loop(0, chunk // step)
-        def _(i):
-            here = pl.ds(pl.multiple_of(i * step, step), step)
-            x_hi[here], x_lo[here] = split(stage[here])
-
-        width = tile_of(lines, 256)
-
-        @pl.loop(0, lines // width)
+        width = tile_of(buses, 1024)
+        turned[...] = jnp.zeros_like(turned)
+
+        @pl.loop(0, buses // width)
         def _(n):
             here = pl.ds(pl.multiple_of(n * width, width), width)
-            flows[s, :, here] = dot3(
-                x_hi[...], x_lo[...], s_hi[here], s_lo[here], ((1,), (1,))
-            )
+            x_hi, x_lo = split(stage[:, here])
+            turned[...] += dot3(s_hi[:, here], s_lo[:, here], x_hi, x_lo, ((1,), (1,)))
+
+        step = tile_of(lines, 128)
+
+        @pl.loop(0, lines // step)
+        def _(n):
+            here = pl.ds(pl.multiple_of(n * step, step), step)
+            flows[s, :, here] = turned[here].T
 
         for r in range(1, bus_count):
             flow_copy(s, r).start()
 
-    def core_copy(s, k):
-        return pltpu.make_async_remote_copy(
-            src_ref=part.at[2 * k + 1 - c], dst_ref=from_core.at[s, k],
-            send_sem=rc_send.at[s, k], recv_sem=rc_recv.at[s, k],
+    half = buses // 2
+
+    def columns(h):
+        return pl.ds(h * half, half)
+
+    def core_copy(s, k, h):
+        return pltpu.make_async_remote_copy(
+            src_ref=part.at[2 * k + 1 - c, :, columns(h)],
+            dst_ref=from_core.at[s, k, :, columns(h)],
+            send_sem=rc_send.at[s, k, h], recv_sem=rc_recv.at[s, k, h],
             device_id=sibling, device_id_type=MESH,
         )
 
-    def x_copy(s):
-        return pltpu.make_async_remote_copy(
-            src_ref=from_core.at[s, 1 - x], dst_ref=from_x.at[s],
-            send_sem=rx_send.at[s], recv_sem=rx_recv.at[s],
+    def x_copy(s, h):
+        return pltpu.make_async_remote_copy(
+            src_ref=from_core.at[s, 1 - x, :, columns(h)],
+            dst_ref=from_x.at[s, :, columns(h)],
+            send_sem=rx_send.at[s, h], recv_sem=rx_recv.at[s, h],
             device_id=across, device_id_type=MESH,
         )
 
-    def z_copy(s):
-        plane = plane_of(s)
-        return pltpu.make_async_remote_copy(
-            src_ref=from_x.at[s], dst_ref=from_z.at[z],
-            send_sem=rz_send.at[s], recv_sem=rz_recv.at[z],
-            device_id=at(plane, x, c), device_id_type=MESH,
+    def z_copy(s, h, target, slot):
+        return pltpu.make_async_remote_copy(
+            src_ref=from_x.at[s, :, columns(h)], dst_ref=from_z.at[slot, :, columns(h)],
+            send_sem=rz_send.at[s, h], recv_sem=rz_recv.at[slot, h],
+            device_id=at(target, x, c), device_id_type=MESH,
         )
 
     def second_product(s):
@@ -194,45 +200,69 @@
             )
             a_hi[here], a_lo[here] = split(adjoint)
 
-        width = tile_of(buses, 512)
-
-        @pl.loop(0, buses // width)
+    def second_half(s, h):
+        width = tile_of(half, 512)
+
+        @pl.loop(0, half // width)
         def _(n):
-            here = pl.ds(pl.multiple_of(n * width, width), width)
+            here = pl.ds(pl.multiple_of(h * half + n * width, width), width)
             value = dot3(a_hi[...], a_lo[...], s_hi[:, here], s_lo[:, here], ((1,), (0,)))
             for block in range(4):
                 part[block, :, here] = value[block * hours : (block + 1) * hours]
 
         for k in range(2):
-            core_copy(s, k).start()
-
-    def add_to(ref, *others):
+            core_copy(s, k, h).start()
+
+    def add_to(ref, other, h=None):
         step = tile_of(hours, 8)
+        cols = pl.ds(0, buses) if h is None else columns(h)
 
         @pl.loop(0, hours // step)
         def _(i):
             here = pl.ds(pl.multiple_of(i * step, step), step)
-            total = ref[here]
-            for other in others:
-                total = total + other[here]
-            ref[here] = total
-
-    def reduce_across(s):
+            ref[here, cols] += other[here, cols]
+
+    def reduce_across(s, h):
         for k in range(2):
-            core_copy(s, k).wait_recv()
-        add_to(from_core.at[s, 1 - x], part.at[2 * (1 - x) + c])
-        x_copy(s).start()
-        add_to(from_core.at[s, x], part.at[me])
-        for k in range(2):
-            core_copy(s, k).wait_send()
+            core_copy(s, k, h).wait_recv()
+        add_to(from_core.at[s, 1 - x], part.at[2 * (1 - x) + c], h)
+        x_copy(s, h).start()
+        add_to(from_core.at[s, x], part.at[me], h)
 
     def reduce_along(s):
-        x_copy(s).wait_recv()
-        add_to(from_x.at[s], from_core.at[s, x])
-
-        @pl.when(s > 0)
-        def _():
-            z_copy(s).start()
+        for h in range(2):
+            x_copy(s, h).wait_recv()
+            add_to(from_x.at[s], from_core.at[s, x], h)
+
+            @pl.when(s > 0)
+            def _():
+                z_copy(s, h, plane_of(s), z).start()
+
+    def stat_copy(step, r=1):
+        pair = 2 * x
+        src, target = (
+            (all_stats.at[z, pl.ds(me, 1)], sibling),
+            (all_stats.at[z, pl.ds(pair, 2)], across),
+            (all_stats.at[z], at((z + r) % planes, x, c)),
+        )[step]
+        return pltpu.make_async_remote_copy(
+            src_ref=src, dst_ref=src,
+            send_sem=st_send.at[step + r - 1], recv_sem=st_recv.at[step + r - 1],
+            device_id=target, device_id_type=MESH,
+        )
+
+    def stat_arrival(step, r=1):
+        plane = (z - r + planes) % planes
+        ref = (
+            all_stats.at[z, pl.ds(2 * x + 1 - c, 1)],
+            all_stats.at[z, pl.ds(2 * (1 - x), 2)],
+            all_stats.at[plane],
+        )[step]
+        return pltpu.make_async_remote_copy(
+            src_ref=ref, dst_ref=ref,
+            send_sem=st_send.at[step + r - 1], recv_sem=st_recv.at[step + r - 1],
+            device_id=sibling, device_id_type=MESH,
+        )
 
     barrier = pltpu.get_barrier_semaphore()
     mine = pltpu.make_async_copy(inj, gathered.at[z, rows(me)], local_sem.at[0])
@@ -284,7 +314,13 @@
         def _():
             s = (t - 1) % planes
             second_product(s)
-            reduce_across(s)
+            second_half(s, 0)
+            second_half(s, 1)
+            reduce_across(s, 0)
+            reduce_across(s, 1)
+            for h in range(2):
+                for k in range(2):
+                    core_copy(s, k, h).wait_send()
 
         @pl.when(t >= 3)
         def _():
@@ -293,11 +329,8 @@
     total = from_x.at[0]
     for r in range(1, planes):
         other = (z + r) % planes
-        pltpu.make_async_remote_copy(
-            src_ref=from_x.at[0], dst_ref=from_z.at[other],
-            send_sem=rz_send.at[0], recv_sem=rz_recv.at[other],
-            device_id=at(other, x, c), device_id_type=MESH,
-        ).wait_recv()
+        for h in range(2):
+            z_copy(0, h, other, other).wait_recv()
         add_to(total, from_z.at[other])
     store = pltpu.make_async_copy(total, out, local_sem.at[0])
     store.start()
@@ -308,8 +341,8 @@
     @pl.loop(0, buses // width)
     def _(n):
         here = pl.ds(pl.multiple_of(n * width, width), width)
-        place = n * width + lax.broadcasted_iota(jnp.int32, (width, source.shape[1]), 0)
-        chosen = jnp.where(place == local_bus[...], 1.0, 0.0).astype(BF16)
+        place = lax.broadcasted_iota(jnp.int32, (width, source.shape[1]), 0)
+        chosen = jnp.where(place + (bus * buses + n * width) == storage_bus[...], 1.0, 0.0).astype(BF16)
         left = total[:, here]
         for _ in range(3):
             high = left.astype(BF16)
@@ -324,12 +357,33 @@
         costate = discharge[...] * source[pl.ds(t, 1), :] + carry
         return (keep * costate, keep * gain, fixed + costate * weight, slope + gain * weight)
 
+    all_stats[z, me] = jnp.zeros(all_stats.shape[2:], F32)
     zero = jnp.zeros((1, source.shape[1]), F32)
     done = lax.fori_loop(0, hours, hour_back, (zero, zero + 1.0, zero, zero))
-    stats[...] = jnp.zeros_like(stats)
     for i in range(4):
-        stats[i : i + 1, :] = done[i]
-
+        all_stats[z, me, i : i + 1, :] = done[i]
+    for step in range(2):
+        stat_copy(step).start()
+        stat_arrival(step).wait_recv()
+    for r in range(1, planes):
+        stat_copy(2, r).start()
+    for r in range(1, planes):
+        stat_arrival(2, r).wait_recv()
+
+    def block_back(i, carried):
+        carry, total = carried
+        block = 4 * planes - 1 - i
+        offset, gain, fixed, slope = (
+            all_stats[block // 4, block % 4, row : row + 1, :] for row in range(4)
+        )
+        return (offset + gain * carry, total + (fixed + slope * carry))
+
+    sums = lax.fori_loop(0, 4 * planes, block_back, (zero, zero))
+    size[...] = sums[1] / math.sqrt(4 * planes * hours)
+    for step in range(2):
+        stat_copy(step).wait_send()
+    for r in range(1, planes):
+        stat_copy(2, r).wait_send()
     store.wait()
 
     @pl.loop(0, planes)
@@ -349,11 +403,13 @@
             to_sibling(plane, k).wait_send()
         for r in range(1, bus_count):
             flow_copy(s, r).wait_send()
-        x_copy(s).wait_send()
+        for h in range(2):
+            x_copy(s, h).wait_send()
 
         @pl.when(s > 0)
         def _():
-            z_copy(s).wait_send()
+            for h in range(2):
+                z_copy(s, h, plane_of(s), z).wait_send()
 
 
 def on_device(
@@ -365,14 +421,13 @@
     stores = retention.shape[1]
     chunk = 4 * hours
     all_hours = chunk * planes
-    local_bus = storage_bus - lax.axis_index("bus") * buses
     hbm, vmem = pl.BlockSpec(memory_space=pl.ANY), pl.BlockSpec(memory_space=pltpu.VMEM)
     dma = pltpu.SemaphoreType.DMA
-    bus_adjoint, stats, _ = pl.pallas_call(
+    bus_adjoint, size_grad, _ = pl.pallas_call(
         functools.partial(kernel, planes, bus_count),
         out_shape=(
             jax.ShapeDtypeStruct((hours, buses), F32),
-            jax.ShapeDtypeStruct((8, stores), F32),
+            jax.ShapeDtypeStruct((1, stores), F32),
             jax.ShapeDtypeStruct((planes, chunk, buses), F32),
         ),
         in_specs=[hbm, hbm, hbm, vmem, vmem, vmem, vmem, vmem],
@@ -381,8 +436,7 @@
             pltpu.VMEM((lines, buses), BF16),
             pltpu.VMEM((lines, buses), BF16),
             pltpu.VMEM((chunk, buses), F32),
-            pltpu.VMEM((chunk, buses), BF16),
-            pltpu.VMEM((chunk, buses), BF16),
+            pltpu.VMEM((lines, chunk), F32),
             pltpu.VMEM((planes, chunk, lines), F32),
             pltpu.VMEM((planes, bus_count - 1, chunk, lines), F32),
             pltpu.VMEM((chunk, lines), BF16),
@@ -393,14 +447,16 @@
             pltpu.VMEM((planes, hours, buses), F32),
             pltpu.VMEM((planes, hours, buses), F32),
             pltpu.VMEM((hours, stores), F32),
+            pltpu.VMEM((planes, 4, 8, stores), F32),
             dma((1,)),
             dma((2, planes)), dma((planes,)),
             dma((planes,)), dma((planes,)),
             dma((2, planes)), dma((2, planes)),
             dma((planes, bus_count - 1)), dma((planes, bus_count - 1)),
+            dma((planes, 2, 2)), dma((planes, 2, 2)),
             dma((planes, 2)), dma((planes, 2)),
-            dma((planes,)), dma((planes,)),
-            dma((planes,)), dma((planes,)),
+            dma((planes, 2)), dma((planes, 2)),
+            dma((planes + 1,)), dma((planes + 1,)),
         ],
         compiler_params=pltpu.CompilerParams(
             collective_id=0, has_side_effects=True, vmem_limit_bytes=60 * 2**20
@@ -412,16 +468,9 @@
         ),
     )(
         injections, shift_factors, line_rating, retention, discharge[None], profile,
-        local_bus[None], online_hour[None],
+        storage_bus[None], online_hour[None],
     )
-    everyone = lax.all_gather(stats, "line")
-    carried = jnp.zeros((stores,), F32)
-    total = jnp.zeros((stores,), F32)
-    for block in reversed(range(4 * planes)):
-        offset, gain, fixed, slope = (everyone[block, i] for i in range(4))
-        total = total + (fixed + slope * carried)
-        carried = offset + gain * carried
-    return (bus_adjoint, total / math.sqrt(all_hours))
+    return (bus_adjoint, size_grad[0])
 
 
 def solution(mesh):

time: 307 us -> 292 us (0.951)
  blocking collectives: 26.4 us -> 0 us
  Pallas kernels: 275 us -> 287 us
    all_gather x1 -> x0, blocking collectives: 26.4 us -> none  [on_device(): everyone = lax.all_gather(stats, 'line')]
    pallas_call x1, Pallas kernels: 275 us -> 287 us  [on_device(): pl.pallas_call(functools.partial(kernel, planes, bus_count), out_shape=(j...]
where the time goes in v2:
time: 292 us; the launch traced here: 291 us
  Pallas kernels  287 us (98%)
  local copies, waits for them, and re-layouts  3.45 us (1%)
    pallas_call x1, Pallas kernels, on_device(): pl.pallas_call(functools.partial(kernel, planes, bus_count), out_shape=(j...  287 us

profile of v2, /device:TPU:0, one launch (start us, length us, event | category | flops | bytes accessed | tf_op | source)
XLA Modules:
  0.0 291.0 jit_solution(15608262227869221266)
XLA Ops:
  0.6 286.9 %shard_map.95 = (f32[64,4096]{1,0:T(8,128)}, f32[1,128]{1,0:T(1,128)}, f32[4,256,4096]{2,1,0:T(8,128)}) custom-call(f32[64,4096]{1,0:T(8,128)} %inj.1, f32[1024,4096]{1,0:T(8,128)} %factors.1, s32[1024,1024]{1,0:T(8,128)} %rating.1, f32[64,128]{1,0:T(8,128)} %retention.1, f32[1,128]{1,0:T(1,128)} %bitcast.4, f32[64,128]{1,0:T(8,128)} %profile.1, ...), custom_call_target="tpu_custom_call" | custom-call | flops 51539607552 | bytes 37748736 | tf_op jit(solution)/shard_map/pallas_call | solution.py:426
  287.6 2.3 copy.12
  289.9 1.2 copy.13

commit v3 on v2

--- a/solution.py
+++ b/solution.py
@@ -51,11 +51,10 @@
     sibling, across = at(z, x, 1 - c), at(z, 1 - x, c)
 
     def plane_of(s):
-        both = jnp.minimum(z, planes - 1 - z)
-        away = (s + 1) // 2
-        near = jnp.where(s % 2 == 1, z - away, z + away)
-        far = jnp.where(z < planes - 1 - z, s, planes - 1 - s)
-        return jnp.where(s <= 2 * both, near, far)
+        above = planes - 1 - z
+        up = jnp.where(s <= above, z + s, z - (s - above))
+        down = jnp.where(s <= z, z - s, s)
+        return jnp.where(z <= above, up, down)
 
     def rows(block):
         return pl.ds(pl.multiple_of(block * hours, hours), hours)
@@ -94,10 +93,8 @@
     def goes_down(plane):
         return (plane >= z) & (z > 0)
 
-    def forward(s):
-        plane = plane_of(s)
-
-        @pl.when(s > 0)
+    def pass_on(plane):
+        @pl.when(plane != z)
         def _():
             along_z(plane, 0, z).wait_recv()
 
@@ -109,8 +106,16 @@
         def _():
             along_z(plane, 1, z - 1).start()
 
-        to_across(plane).start()
         to_sibling(plane, 0).start()
+
+    def pass_on_at(distance):
+        @pl.when(z - distance >= 0)
+        def _():
+            pass_on(z - distance)
+
+        @pl.when(z + distance < planes)
+        def _():
+            pass_on(z + distance)
 
     def forward_across(s):
         plane = plane_of(s)
@@ -279,7 +284,8 @@
         )
     mine.wait()
     pl.semaphore_wait(barrier, planes + bus_count)
-    forward(0)
+    pass_on(z)
+    to_across(z).start()
 
     group = tile_of(lines, chunk)
 
@@ -303,7 +309,8 @@
     def _(t):
         @pl.when(t + 1 < planes)
         def _():
-            forward(t + 1)
+            pass_on_at(t + 1)
+            to_across(plane_of(t + 1)).start()
 
         @pl.when(t < planes)
         def _():

time: 292 us -> 281 us (0.962)
  Pallas kernels: 287 us -> 276 us
    pallas_call x1, Pallas kernels: 287 us -> 276 us  [on_device(): pl.pallas_call(functools.partial(kernel, planes, bus_count), out_shape=(j...]
where the time goes in v3:
time: 281 us; the launch traced here: 280 us
  Pallas kernels  276 us (98%)
  local copies, waits for them, and re-layouts  3.45 us (1%)
    pallas_call x1, Pallas kernels, on_device(): pl.pallas_call(functools.partial(kernel, planes, bus_count), out_shape=(j...  276 us

profile of v3, /device:TPU:0, one launch (start us, length us, event | category | flops | bytes accessed | tf_op | source)
XLA Modules:
  0.0 280.4 jit_solution(15082845626663182251)
XLA Ops:
  0.6 276.3 %shard_map.95 = (f32[64,4096]{1,0:T(8,128)}, f32[1,128]{1,0:T(1,128)}, f32[4,256,4096]{2,1,0:T(8,128)}) custom-call(f32[64,4096]{1,0:T(8,128)} %inj.1, f32[1024,4096]{1,0:T(8,128)} %factors.1, s32[1024,1024]{1,0:T(8,128)} %rating.1, f32[64,128]{1,0:T(8,128)} %retention.1, f32[1,128]{1,0:T(1,128)} %bitcast.4, f32[64,128]{1,0:T(8,128)} %profile.1, ...), custom_call_target="tpu_custom_call" | custom-call | flops 51539607552 | bytes 37748736 | tf_op jit(solution)/shard_map/pallas_call | solution.py:433
  276.9 2.3 copy.12
  279.2 1.2 copy.13

commit v4 on v3

--- a/solution.py
+++ b/solution.py
@@ -17,11 +17,8 @@
     return high, (value - high.astype(F32)).astype(BF16)
 
 
-def dot3(a_hi, a_lo, b_hi, b_lo, dims):
-    dot = functools.partial(
-        lax.dot_general, dimension_numbers=(dims, ((), ())), preferred_element_type=F32
-    )
-    return dot(a_hi, b_hi) + (dot(a_hi, b_lo) + dot(a_lo, b_hi))
+def dot(a, b, dims):
+    return lax.dot_general(a, b, (dims, ((), ())), preferred_element_type=F32)
 
 
 def tile_of(width, most):
@@ -32,7 +29,7 @@
     planes, bus_count,
     inj, factors, rating, retention, discharge, profile, storage_bus, online,
     out, size, gathered,
-    s_hi, s_lo, stage, turned, flows, flows_in, a_hi, a_lo, limit, part,
+    s_hi, s_lo, stage, turned, flows, flows_in, adjoint, limit, part,
     from_core, from_x, from_z, source, all_stats,
     local_sem,
     gz_send, gz_recv, gx_send, gx_recv, gc_send, gc_recv,
@@ -143,7 +140,9 @@
         def _(n):
             here = pl.ds(pl.multiple_of(n * width, width), width)
             x_hi, x_lo = split(stage[:, here])
-            turned[...] += dot3(s_hi[:, here], s_lo[:, here], x_hi, x_lo, ((1,), (1,)))
+            both = dot(s_hi[:, here], jnp.concatenate([x_hi, x_lo], axis=0), ((1,), (1,)))
+            rest = dot(s_lo[:, here], x_hi, ((1,), (1,)))
+            turned[...] += both[:, :chunk] + (both[:, chunk:] + rest)
 
         step = tile_of(lines, 128)
 
@@ -200,10 +199,11 @@
             for r in range(1, bus_count):
                 total = total + flows_in[s, r - 1, here]
             bound = limit[here].astype(F32) * 0.01
-            adjoint = jnp.where(
+            excess = jnp.where(
                 total > bound, total - bound, jnp.where(total < -bound, total + bound, 0.0)
             )
-            a_hi[here], a_lo[here] = split(adjoint)
+            below = pl.ds(pl.multiple_of(chunk + i * step, step), step)
+            adjoint[here], adjoint[below] = split(excess)
 
     def second_half(s, h):
         width = tile_of(half, 512)
@@ -211,7 +211,9 @@
         @pl.loop(0, half // width)
         def _(n):
             here = pl.ds(pl.multiple_of(h * half + n * width, width), width)
-            value = dot3(a_hi[...], a_lo[...], s_hi[:, here], s_lo[:, here], ((1,), (0,)))
+            both = dot(adjoint[...], s_hi[:, here], ((1,), (0,)))
+            rest = dot(adjoint[:chunk], s_lo[:, here], ((1,), (0,)))
+            value = both[:chunk] + (both[chunk:] + rest)
             for block in range(4):
                 part[block, :, here] = value[block * hours : (block + 1) * hours]
 
@@ -305,7 +307,7 @@
             there = pl.ds(pl.multiple_of(i * group + j * step, step), step)
             s_hi[there], s_lo[there] = split(stage[here])
 
-    @pl.loop(0, planes + 3)
+    @pl.loop(0, planes + 2)
     def _(t):
         @pl.when(t + 1 < planes)
         def _():
@@ -317,9 +319,9 @@
             forward_across(t)
             first_product(t)
 
-        @pl.when((t >= 2) & (t < planes + 2))
-        def _():
-            s = (t - 1) % planes
+        @pl.when((t >= 1) & (t < planes + 1))
+        def _():
+            s = t - 1
             second_product(s)
             second_half(s, 0)
             second_half(s, 1)
@@ -329,9 +331,9 @@
                 for k in range(2):
                     core_copy(s, k, h).wait_send()
 
-        @pl.when(t >= 3)
-        def _():
-            reduce_along((t - 2) % planes)
+        @pl.when(t >= 2)
+        def _():
+            reduce_along(t - 2)
 
     total = from_x.at[0]
     for r in range(1, planes):
@@ -446,8 +448,7 @@
             pltpu.VMEM((lines, chunk), F32),
             pltpu.VMEM((planes, chunk, lines), F32),
             pltpu.VMEM((planes, bus_count - 1, chunk, lines), F32),
-            pltpu.VMEM((chunk, lines), BF16),
-            pltpu.VMEM((chunk, lines), BF16),
+            pltpu.VMEM((2 * chunk, lines), BF16),
             pltpu.VMEM((chunk, lines), jnp.int32),
             pltpu.VMEM((4, hours, buses), F32),
             pltpu.VMEM((planes, 2, hours, buses), F32),

time: 281 us -> 300 us (1.068)
  Pallas kernels: 276 us -> 295 us
    pallas_call x1, Pallas kernels: 276 us -> 295 us  [on_device(): pl.pallas_call(functools.partial(kernel, planes, bus_count), out_shape=(j...]
where the time goes in v4:
time: 300 us; the launch traced here: 299 us
  Pallas kernels  295 us (98%)
  local copies, waits for them, and re-layouts  3.45 us (1%)
    pallas_call x1, Pallas kernels, on_device(): pl.pallas_call(functools.partial(kernel, planes, bus_count), out_shape=(j...  295 us

profile of v4, /device:TPU:0, one launch (start us, length us, event | category | flops | bytes accessed | tf_op | source)
XLA Modules:
  0.0 299.1 jit_solution(5870392614805144741)
XLA Ops:
  0.6 295.0 %shard_map.95 = (f32[64,4096]{1,0:T(8,128)}, f32[1,128]{1,0:T(1,128)}, f32[4,256,4096]{2,1,0:T(8,128)}) custom-call(f32[64,4096]{1,0:T(8,128)} %inj.1, f32[1024,4096]{1,0:T(8,128)} %factors.1, s32[1024,1024]{1,0:T(8,128)} %rating.1, f32[64,128]{1,0:T(8,128)} %retention.1, f32[1,128]{1,0:T(1,128)} %bitcast.4, f32[64,128]{1,0:T(8,128)} %profile.1, ...), custom_call_target="tpu_custom_call" | custom-call | flops 51539607552 | bytes 37748736 | tf_op jit(solution)/shard_map/pallas_call | solution.py:435
  295.7 2.3 copy.12
  298.0 1.2 copy.13

commit v5 on v3

--- a/solution.py
+++ b/solution.py
@@ -305,7 +305,7 @@
             there = pl.ds(pl.multiple_of(i * group + j * step, step), step)
             s_hi[there], s_lo[there] = split(stage[here])
 
-    @pl.loop(0, planes + 3)
+    @pl.loop(0, planes + 4)
     def _(t):
         @pl.when(t + 1 < planes)
         def _():
@@ -315,23 +315,30 @@
         @pl.when(t < planes)
         def _():
             forward_across(t)
-            first_product(t)
-
-        @pl.when((t >= 2) & (t < planes + 2))
-        def _():
-            s = (t - 1) % planes
-            second_product(s)
-            second_half(s, 0)
-            second_half(s, 1)
+
+        @pl.when((t >= 3) & (t < planes + 3))
+        def _():
+            s = (t - 2) % planes
             reduce_across(s, 0)
             reduce_across(s, 1)
             for h in range(2):
                 for k in range(2):
                     core_copy(s, k, h).wait_send()
 
-        @pl.when(t >= 3)
-        def _():
-            reduce_along((t - 2) % planes)
+        @pl.when(t >= 4)
+        def _():
+            reduce_along((t - 3) % planes)
+
+        @pl.when(t < planes)
+        def _():
+            first_product(t)
+
+        @pl.when((t >= 2) & (t < planes + 2))
+        def _():
+            s = (t - 1) % planes
+            second_product(s)
+            second_half(s, 0)
+            second_half(s, 1)
 
     total = from_x.at[0]
     for r in range(1, planes):

time: 281 us -> 279 us (level)
  no operation moved by 1% of the time
where the time goes in v5:
time: 279 us
  Pallas kernels  274 us (98%)
  local copies, waits for them, and re-layouts  3.45 us (1%)
    pallas_call x1, Pallas kernels, on_device(): pl.pallas_call(functools.partial(kernel, planes, bus_count), out_shape=(j...  274 us

profile of v5, /device:TPU:0, one launch (start us, length us, event | category | flops | bytes accessed | tf_op | source)
XLA Modules:
  0.0 278.5 jit_solution(6047214274154795701)
XLA Ops:
  0.6 274.4 %shard_map.95 = (f32[64,4096]{1,0:T(8,128)}, f32[1,128]{1,0:T(1,128)}, f32[4,256,4096]{2,1,0:T(8,128)}) custom-call(f32[64,4096]{1,0:T(8,128)} %inj.1, f32[1024,4096]{1,0:T(8,128)} %factors.1, s32[1024,1024]{1,0:T(8,128)} %rating.1, f32[64,128]{1,0:T(8,128)} %retention.1, f32[1,128]{1,0:T(1,128)} %bitcast.4, f32[64,128]{1,0:T(8,128)} %profile.1, ...), custom_call_target="tpu_custom_call" | custom-call | flops 51539607552 | bytes 37748736 | tf_op jit(solution)/shard_map/pallas_call | solution.py:440
  275.1 2.3 copy.12
  277.4 1.2 copy.13
